TPU v7x, 32 devices: a whole 2x2x4 slice. The times are simulated.
32 devices in a mesh: grp: 2 (over y), ia: 4 (over x, core), ja: 4 (over z).
Axes of the slice: x: 2, y: 2, z: 4, core: 2. Of those that a mesh axis runs over, the one named last changes fastest.
Arguments:
- amplitudes: float32 [16, 8, 160, 160], P(('grp', 'ia'), 'ja'), parts along dimension 0, may hold values from -3 to 3
- integrals: float32 [16, 8, 160, 160], P(('grp', 'ia'), 'ja'), parts along dimension 0, may hold values from -6 to 6
- row_intersection: float32 [16, 8, 8, 160, 160], P(('grp', 'ia'), 'ja'), parts along dimension 0, as said below
- column_intersection: float32 [16, 8, 8, 160, 160], P(('grp', 'ia'), 'ja'), parts along dimension 0, as said below
- row_tiles: int32 [16, 8], P(('grp', 'ia')), parts along dimension 0, may hold values from 0 to 7, as said below
- row_coupling: float32 [16, 8], P(('grp', 'ia')), parts along dimension 0, may hold values from 0.02 to 0.12
- row_counts: int32 [16], P(('grp', 'ia')), parts along dimension 0, may hold values from 1 to 8, as said below
- column_tiles: int32 [16, 8], P(('grp', 'ja')), parts along dimension 0, may hold values from 0 to 7, as said below
- column_coupling: float32 [16, 8], P(('grp', 'ja')), parts along dimension 0, may hold values from 0.02 to 0.12
- column_counts: int32 [16], P(('grp', 'ja')), parts along dimension 0, may hold values from 1 to 8, as said below
- virtual_energy: float32 [16, 8, 160], P(('grp', 'ia'), 'ja'), parts along dimension 0, may hold values from 0.5 to 3
- first_energy: float32 [16], P(('grp', 'ia')), parts along dimension 0, may hold values from -1.5 to -0.3
- second_energy: float32 [16], P(('grp', 'ja')), parts along dimension 0, may hold values from -1.5 to -0.3
Outputs:
- new_amplitudes: float32 [16, 8, 160, 160], P(('grp', 'ia'), 'ja'), parts along dimension 0
- last_residual: float32 [16, 8, 160, 160], P(('grp', 'ia'), 'ja'), parts along dimension 0
There are 2 independent parts, one for each index of `grp`. A program takes and returns all parts, laid end to end along the dimension named above; each array names one. Nothing has to cross between parts.
Inputs may be any that keep to these rules, and one draw needn't show every extreme that they name: `row_tiles`: each row holds 8 different first-fragment orbitals. `column_tiles`: each row holds 8 different second-fragment orbitals. `row_counts`: some orbital has all 8 slots live. `column_counts`: some orbital has all 8 slots live. `row_intersection`: identity plus an independent perturbation of full rank. `column_intersection`: identity plus an independent perturbation of full rank.
All inputs are finite; a program needn't handle non-finite values.
Results may differ from a plain program's by a relative error of at most 0.00017.
Values sent between devices are 32-bit elements; how exact they have to be, the bound alone decides.
A program may use at most 128 MiB of HBM per device.

v0:
```python
import functools

import jax
import jax.numpy as jnp
from jax import lax
from jax.experimental import pallas as pl
from jax.experimental.pallas import tpu as pltpu
from jax.sharding import PartitionSpec as P

ITERS = 2
LANES = 128
MESH = pl.DeviceIdType.MESH
BF16 = jnp.bfloat16
F32 = jnp.float32


def split(x):
    high = x.astype(BF16)
    return high, (x - high.astype(F32)).astype(BF16)


def dot(a, b, b_side):
    return lax.dot_general(a, b, (((1,), (b_side,)), ((), ())), preferred_element_type=F32)


def product3(a, b_high, b_low, b_side):
    rows = a.shape[0]
    a_high, a_low = split(a)
    both = dot(jnp.concatenate([a_high, a_low], axis=0), b_high, b_side)
    return both[:rows] + both[rows:] + dot(a_high, b_low, b_side)


class Wire:
    def __init__(self, tiles, size):
        self.tiles, self.size = tiles, size
        self.full = size // LANES
        self.rest = size % LANES
        self.per = LANES // self.rest if self.rest else tiles
        self.shared = -(-tiles // self.per) if self.rest else 0
        self.planes = tiles * self.full + self.shared
        half = tiles // 2 * self.full
        self.chunks = ((0, half), (half, self.planes)) if half else ((0, self.planes),)


def events_of(ni, nj, nia, nja):
    cores = 2 if nia % 2 == 0 else 1
    places = nia // cores
    groups = [[("row", "own", 0, 0), ("col", "own", 0, 0)]]
    if cores == 2:
        groups.append([("row", "core", 0, 1)])
    for t in range(1, max(places, nja)):
        group = []
        if t < nja:
            group += [("col", "up", t, 0), ("col", "down", t, 0)]
        if t < places:
            group.append(("row", "place", t, 0))
            if cores == 2:
                group.append(("row", "core", t, 1))
        groups.append(group)
    return cores, places, groups


def kernel(
    nia, nja, wire,
    amp, integ, row_tiles, row_coup, row_counts, col_tiles, col_coup, col_counts, virt, first, second,
    row_s, col_s,
    new_amp, last_res,
    s_all, buf, cur, acc, den, t_high, t_low, slot_tab, weight_tab, load_sem, send_sem, recv_sem,
):
    ni, nj, size, _ = amp.shape
    pairs = ni * nj
    slots = row_tiles.shape[1]
    cores, places, groups = events_of(ni, nj, nia, nja)
    me_a, me_z = lax.axis_index("ia"), lax.axis_index("ja")
    place, core = me_a // cores, me_a % cores
    chunks = wire.chunks
    own_norb = (nia * ni, nja * nj)

    loads = [
        pltpu.make_async_copy(row_s, s_all.at[0], load_sem.at[0]),
        pltpu.make_async_copy(col_s, s_all.at[1], load_sem.at[1]),
    ]
    for load in loads:
        load.start()

    def sibling():
        return {"ia": place * cores + (core + 1) % cores}

    def placed(step):
        return {"ia": ((place + step) % places) * cores + core}

    has_up, has_down = me_z < nja - 1, me_z > 0

    barrier = pltpu.get_barrier_semaphore()

    def greet(device):
        pl.semaphore_signal(barrier, inc=1, device_id=device, device_id_type=MESH)

    if cores == 2:
        greet(sibling())
    for step in range(1, places):
        greet(placed(step))
    if nja > 1:
        @pl.when(has_up)
        def _():
            greet({"ja": me_z + 1})

        @pl.when(has_down)
        def _():
            greet({"ja": me_z - 1})

    flat = [event for group in groups for event in group]
    info = []
    next_buffer = 1
    where = {}
    for event in flat:
        kind, how, step, flip = event
        if how == "own":
            index, here = 0, jnp.bool_(True)
        else:
            index, here = next_buffer, jnp.bool_(True)
            next_buffer += 1
        if how == "up":
            source, here = me_z - step, me_z - step >= 0
        elif how == "down":
            source, here = me_z + step, me_z + step < nja
        elif kind == "col":
            source = me_z
        else:
            source = ((place + places - step) % places) * cores + (core + flip) % cores
        where[(how, step)] = index
        info.append((0 if kind == "row" else 1, index, source, here))

    def copy(it, number, source_index, target_index, chunk, device):
        low, high = chunks[chunk]
        return pltpu.make_async_remote_copy(
            src_ref=buf.at[it, source_index, pl.ds(low, high - low)],
            dst_ref=buf.at[it, target_index, pl.ds(low, high - low)],
            send_sem=send_sem.at[it, number * len(chunks) + chunk],
            recv_sem=recv_sem.at[it, target_index * len(chunks) + chunk],
            device_id=device,
            device_id_type=MESH,
        )

    sends = []
    if nja > 1:
        for t in range(0, nja - 1):
            source_up = where[("up", t)] if t else 0
            source_down = where[("down", t)] if t else 0
            sends.append((("up", t) if t else ("own", 0), source_up, where[("up", t + 1)], {"ja": me_z + 1}, has_up & (me_z - t >= 0)))
            sends.append((("down", t) if t else ("own", 0), source_down, where[("down", t + 1)], {"ja": me_z - 1}, has_down & (me_z + t < nja)))
    for t in range(1, places):
        sends.append((("own", 0), 0, where[("place", t)], placed(t), None))
    if cores == 2:
        sends.append((("own", 0), 0, where[("core", 0)], sibling(), None))
        for t in range(1, places):
            sends.append((("place", t), where[("place", t)], where[("core", t)], sibling(), None))
    sends = [(number,) + send for number, send in enumerate(sends)]

    def guarded(condition, act):
        if condition is None:
            act()
        else:
            pl.when(condition)(act)

    def send_after(key, it, chunk):
        for number, after, source_index, target_index, device, condition in sends:
            if after == key:
                guarded(
                    condition,
                    lambda: copy(it, number, source_index, target_index, chunk, device).start(),
                )

    def wait_chunk(it, index, chunk):
        copy(it, 0, index, index, chunk, {"ja": me_z, "ia": me_a}).wait_recv()

    def pack(it, p):
        tile = cur[p]
        for f in range(wire.full):
            buf[it, 0, p * wire.full + f] = tile[:, f * LANES:(f + 1) * LANES]

    def pack_shared(it):
        for plane in range(wire.shared):
            some = [
                cur[p, :, wire.full * LANES:]
                for p in range(plane * wire.per, min(pairs, (plane + 1) * wire.per))
            ]
            room = LANES - len(some) * wire.rest
            if room:
                some.append(jnp.zeros((size, room), F32))
            buf[it, 0, pairs * wire.full + plane] = jnp.concatenate(some, axis=1)

    def send_own(it):
        half = pairs // 2 if len(chunks) == 2 else pairs
        for p in range(half):
            pack(it, p)
        if len(chunks) == 2:
            send_after(("own", 0), it, 0)
            for p in range(half, pairs):
                pack(it, p)
        pack_shared(it)
        send_after(("own", 0), it, len(chunks) - 1)

    for p in range(pairs):
        cur[p] = amp[p // nj, p % nj]
    greeted = (1 if cores == 2 else 0) + places - 1
    if nja > 1:
        greeted = greeted + has_up.astype(jnp.int32) + has_down.astype(jnp.int32)
    pl.semaphore_wait(barrier, greeted)
    send_own(0)

    for kind, (tiles, coup, counts, count) in enumerate(
        ((row_tiles, row_coup, row_counts, ni), (col_tiles, col_coup, col_counts, nj))
    ):
        for a in range(count):
            def fill(k, carry, kind=kind, tiles=tiles, coup=coup, counts=counts, a=a):
                slot, weight = jnp.int32(0), F32(0)
                live = counts[a]
                for l in range(slots):
                    match = tiles[a, l] == k
                    slot = jnp.where(match, jnp.int32(l), slot)
                    weight = jnp.where(match & (l < live), coup[a, l], weight)
                slot_tab[kind, a, k] = slot
                weight_tab[kind, a, k] = weight
                return carry

            lax.fori_loop(0, own_norb[kind], fill, 0)

    rows_of = lax.broadcasted_iota(jnp.int32, (size, size), 0)
    columns_of = lax.broadcasted_iota(jnp.int32, (size, size), 1)
    for p in range(pairs):
        i, j = p // nj, p % nj
        across = virt[i, j:j + 1, :]
        down = jnp.sum(jnp.where(rows_of == columns_of, across, 0.0), axis=1, keepdims=True)
        den[p] = down + across - first[i] - second[j]
        acc[p] = jnp.zeros((size, size), F32)

    for load in loads:
        load.wait()

    def pick(e, values):
        out = values[0]
        for index in range(1, len(values)):
            out = jnp.where(e == index, values[index], out)
        return out

    def one_event(it, e):
        start = 0
        for group in groups:
            arriving = [event for event in group if event[1] != "own"]

            def take(group=arriving, start=start):
                for chunk in range(len(chunks)):
                    for kind, how, step, flip in group:
                        if how == "core" and step:
                            continue
                        here = info[flat.index((kind, how, step, flip))][3]

                        def arrive(how=how, step=step, chunk=chunk):
                            wait_chunk(it, where[(how, step)], chunk)
                            send_after((how, step), it, chunk)

                        guarded(here if how in ("up", "down") else None, arrive)

            if arriving:
                pl.when(e == start)(take)
                for kind, how, step, flip in arriving:
                    if how == "core" and step:
                        @pl.when(e == flat.index((kind, how, step, flip)))
                        def _(step=step):
                            for chunk in range(len(chunks)):
                                wait_chunk(it, where[("core", step)], chunk)
            start += len(group)

        kind = pick(e, [jnp.int32(x[0]) for x in info])
        index = pick(e, [jnp.int32(x[1]) for x in info])
        source = pick(e, [x[2] for x in info])
        here = pick(e, [x[3].astype(jnp.int32) for x in info]) > 0

        @pl.when(here)
        def _():
            for p in range(pairs):
                for f in range(wire.full):
                    lanes = slice(f * LANES, (f + 1) * LANES)
                    t_high[p, :, lanes], t_low[p, :, lanes] = split(buf[it, index, p * wire.full + f])
                if wire.rest:
                    part = buf[it, index, pairs * wire.full + p // wire.per]
                    offset = p % wire.per * wire.rest
                    if offset:
                        part = pltpu.roll(part, LANES - offset, 1)
                    lanes = slice(wire.full * LANES, size)
                    t_high[p, :, lanes], t_low[p, :, lanes] = split(part[:, :wire.rest])

            is_row = kind == 0

            def one_orbital(inner, carry):
                orbital = source * jnp.where(is_row, ni, nj) + inner
                for p in range(pairs):
                    i, j = p // nj, p % nj
                    mine = jnp.where(is_row, i, j)
                    slot = slot_tab[kind, mine, orbital]
                    weight = weight_tab[kind, mine, orbital]
                    tile = jnp.where(is_row, inner * nj + j, i * nj + inner)
                    s = s_all[kind, i, j, slot]
                    s_high, s_low = split(s)
                    x = dot(jnp.concatenate([s_high, s_low], axis=0), t_high[tile], 0)
                    x = x[:size] + x[size:] + dot(s_high, t_low[tile], 0)
                    acc[p] += product3(x * weight, s_high, s_low, 1)
                return carry

            lax.fori_loop(0, ni if ni == nj else jnp.where(is_row, ni, nj), one_orbital, 0)

    def one_iteration(it, carry):
        def step(e, inner):
            one_event(it, e)
            return inner

        lax.fori_loop(0, len(flat), step, 0)

        for p in range(pairs):
            i, j = p // nj, p % nj
            residual = integ[i, j] + den[p] * cur[p] - acc[p]
            last_res[i, j] = residual
            cur[p] = cur[p] - residual / den[p]
            acc[p] = jnp.zeros((size, size), F32)

        @pl.when(it < ITERS - 1)
        def _():
            send_own(it + 1)

        return carry

    lax.fori_loop(0, ITERS, one_iteration, 0)
    for p in range(pairs):
        new_amp[p // nj, p % nj] = cur[p]

    def drain(it, carry):
        for number, after, source_index, target_index, device, condition in sends:
            for chunk in range(len(chunks)):
                guarded(
                    condition,
                    lambda: copy(it, number, source_index, target_index, chunk, device).wait_send(),
                )
        return carry

    lax.fori_loop(0, ITERS, drain, 0)


def local(
    nia, nja,
    amplitudes, integrals, row_intersection, column_intersection, row_tiles, row_coupling, row_counts,
    column_tiles, column_coupling, column_counts, virtual_energy, first_energy, second_energy,
):
    ni, nj, size, _ = amplitudes.shape
    slots = row_tiles.shape[1]
    pairs = ni * nj
    wire = Wire(pairs, size)
    cores, places, groups = events_of(ni, nj, nia, nja)
    buffers = sum(len(group) for group in groups) - 1
    number_sends = 2 * (nja - 1) + (places - 1) + (places if cores == 2 else 0)
    norb = max(nia * ni, nja * nj)
    vmem = pl.BlockSpec(memory_space=pltpu.VMEM)
    smem = pl.BlockSpec(memory_space=pltpu.SMEM)
    anywhere = pl.BlockSpec(memory_space=pl.ANY)
    tile = (pairs, size, size)
    flops = 2 * 2 * 3 * size**3 * pairs * 2 * norb * ITERS
    return pl.pallas_call(
        functools.partial(kernel, nia, nja, wire),
        out_shape=(
            jax.ShapeDtypeStruct(amplitudes.shape, F32),
            jax.ShapeDtypeStruct(amplitudes.shape, F32),
        ),
        in_specs=[vmem, vmem] + [smem] * 6 + [vmem, smem, smem, anywhere, anywhere],
        out_specs=(vmem, vmem),
        scratch_shapes=[
            pltpu.VMEM((2,) + row_intersection.shape, F32),
            pltpu.VMEM((ITERS, buffers, wire.planes, size, LANES), F32),
            pltpu.VMEM(tile, F32),
            pltpu.VMEM(tile, F32),
            pltpu.VMEM(tile, F32),
            pltpu.VMEM(tile, BF16),
            pltpu.VMEM(tile, BF16),
            pltpu.SMEM((2, max(ni, nj), norb), jnp.int32),
            pltpu.SMEM((2, max(ni, nj), norb), F32),
            pltpu.SemaphoreType.DMA((2,)),
            pltpu.SemaphoreType.DMA((ITERS, number_sends * len(wire.chunks))),
            pltpu.SemaphoreType.DMA((ITERS, buffers * len(wire.chunks))),
        ],
        compiler_params=pltpu.CompilerParams(
            collective_id=0, has_side_effects=True, vmem_limit_bytes=60 * 1024 * 1024
        ),
        cost_estimate=pl.CostEstimate(flops=flops, bytes_accessed=2 * row_intersection.size * 4, transcendentals=0),
        name="pair_residual",
    )(
        amplitudes, integrals, row_tiles, row_coupling, row_counts, column_tiles, column_coupling,
        column_counts, virtual_energy, first_energy, second_energy, row_intersection, column_intersection,
    )


def solution(mesh):
    pair = P(("grp", "ia"), "ja", None, None)
    placed = (
        pair,
        pair,
        P(("grp", "ia"), "ja", None, None, None),
        P(("grp", "ia"), "ja", None, None, None),
        P(("grp", "ia"), None),
        P(("grp", "ia"), None),
        P(("grp", "ia")),
        P(("grp", "ja"), None),
        P(("grp", "ja"), None),
        P(("grp", "ja")),
        P(("grp", "ia"), "ja", None),
        P(("grp", "ia")),
        P(("grp", "ja")),
    )
    return jax.shard_map(
        functools.partial(local, mesh.shape["ia"], mesh.shape["ja"]),
        mesh=mesh,
        in_specs=placed,
        out_specs=(pair, pair),
        check_vma=False,
    )
```

profile of v0, /device:TPU:0, one launch (start us, length us, event | category | flops | bytes accessed | tf_op | source)
XLA Modules:
  0.0 68.2 jit_solution(17264681783169780548)
XLA Ops:
  0.6 63.5 %pair_residual.1 = (f32[2,2,160,160]{3,2,1,0:T(8,128)}, f32[2,2,160,160]{3,2,1,0:T(8,128)}) custom-call(f32[2,2,160,160]{3,2,1,0:T(8,128)} %amp.1, f32[2,2,160,160]{3,2,1,0:T(8,128)} %integ.1, s32[2,8]{1,0:T(2,128)} %row_tiles.1, f32[2,8]{1,0:T(2,128)} %row_coup.1, s32[2]{0:T(128)} %row_counts.1, s32[2,8]{1,0:T(2,128)} %col_tiles.1, f32[2,8]{1,0:T(2,128)} %col_coup.1, ...), custom_call_target="tpu_custom_call" | custom-call | flops 6291456000 | bytes 6553600 | tf_op jit(solution)/shard_map/pair_residual/pallas_call | solution.py:367
  64.2 2.0 %copy.17 = f32[2,2,160,160]{3,2,1,0:T(8,128)} copy(f32[2,2,160,160]{3,2,1,0:T(8,128)} %get-tuple-element.4) | data formatting | bytes 819200
  66.2 2.0 %copy.18 = f32[2,2,160,160]{3,2,1,0:T(8,128)} copy(f32[2,2,160,160]{3,2,1,0:T(8,128)} %get-tuple-element.5) | data formatting | bytes 819200
where the time goes:
time: 68.4 us; the launch traced here: 68.2 us
  Pallas kernels  63.5 us (93%)
  local copies, waits for them, and re-layouts  3.96 us (6%)
    pallas_call x1, Pallas kernels, local(): pl.pallas_call(functools.partial(kernel, nia, nja, wire), out_shape=(jax....  63.5 us
    unnamed x2, local copies, waits for them, and re-layouts  3.96 us

commit v1 on v0

v1 whole, which is shorter than its diff:
```python
import functools

import jax
import jax.numpy as jnp
from jax import lax
from jax.experimental import pallas as pl
from jax.experimental.pallas import tpu as pltpu
from jax.sharding import PartitionSpec as P

ITERS = 2
LANES = 128
MESH = pl.DeviceIdType.MESH
BF16 = jnp.bfloat16
F32 = jnp.float32


def split(x):
    high = x.astype(BF16)
    return high, (x - high.astype(F32)).astype(BF16)


def dot(a, b, b_side):
    return lax.dot_general(a, b, (((1,), (b_side,)), ((), ())), preferred_element_type=F32)


def product3(a, b_high, b_low, b_side):
    rows = a.shape[0]
    a_high, a_low = split(a)
    both = dot(jnp.concatenate([a_high, a_low], axis=0), b_high, b_side)
    return both[:rows] + both[rows:] + dot(a_high, b_low, b_side)


class Wire:
    def __init__(self, tiles, size):
        self.tiles, self.size = tiles, size
        self.full = size // LANES
        self.rest = size % LANES
        per = LANES // self.rest if self.rest else 1
        cut = per // tiles if per % tiles == 0 else 1
        self.per, self.cut = per, cut if size % (16 * cut) == 0 else 1
        self.piece = size // self.cut
        self.shared = -(-tiles * self.cut // per) if self.rest else 0
        self.low = tiles * self.full * size
        self.rows = self.low + self.shared * self.piece

    def pieces(self, plane):
        every = [(t, c * self.piece) for t in range(self.tiles) for c in range(self.cut)]
        return every[plane * self.per:(plane + 1) * self.per]


def events_of(chunks, nia, nja):
    cores = 2 if nia % 2 == 0 else 1
    places = nia // cores
    every = range(chunks)
    groups = [[("row", "own", 0, c) for c in every] + [("col", "own", 0, c) for c in every]]
    if cores == 2:
        groups += [[("row", "core", 0, c)] for c in every]
    for t in range(1, max(places, nja)):
        for c in every:
            if t < nja:
                groups.append([("col", "up", t, c), ("col", "down", t, c)])
            if t < places:
                groups.append([("row", "place", t, c)])
        if t < places and cores == 2:
            groups += [[("row", "core", t, c)] for c in every]
    return cores, places, groups


def buffers_of(cores, places, nja):
    keys = [("own", 0)] + [("core", t) for t in range(places) if cores == 2]
    keys += [("place", t) for t in range(1, places)]
    keys += [(how, t) for how in ("up", "down") for t in range(1, nja)]
    return {key: number for number, key in enumerate(keys)}


def kernel(
    nia, nja, wire,
    row_tiles, row_coup, row_counts, col_tiles, col_coup, col_counts, virt, first, second,
    amp, integ, row_s, col_s,
    cur, acc,
    s_all, buf, given, den, t_high, t_low, slot_tab, weight_tab, load_sem, send_sem, recv_sem,
):
    ni, nj, size, _ = amp.shape
    slots = row_tiles.shape[1]
    cores, places, groups = events_of(ni, nia, nja)
    where = buffers_of(cores, places, nja)
    me_a, me_z = lax.axis_index("ia"), lax.axis_index("ja")
    place, core = me_a // cores, me_a % cores
    norbs = (nia * ni, nja * nj)

    loads = [
        pltpu.make_async_copy(amp, cur, load_sem.at[0]),
        pltpu.make_async_copy(row_s, s_all.at[0], load_sem.at[1]),
        pltpu.make_async_copy(col_s, s_all.at[1], load_sem.at[2]),
        pltpu.make_async_copy(integ, given, load_sem.at[3]),
    ]
    for load in loads:
        load.start()

    def sibling():
        return {"ia": place * cores + (core + 1) % cores}

    def placed(step):
        return {"ia": ((place + step) % places) * cores + core}

    has_up, has_down = me_z < nja - 1, me_z > 0

    barrier = pltpu.get_barrier_semaphore()

    def greet(device):
        pl.semaphore_signal(barrier, inc=1, device_id=device, device_id_type=MESH)

    if cores == 2:
        greet(sibling())
    for step in range(1, places):
        greet(placed(step))
    if nja > 1:
        @pl.when(has_up)
        def _():
            greet({"ja": me_z + 1})

        @pl.when(has_down)
        def _():
            greet({"ja": me_z - 1})

    def here_of(how, step):
        if how == "up":
            return me_z - step >= 0
        if how == "down":
            return me_z + step < nja
        return None

    def source_of(kind, how, step):
        if kind == "col":
            return {"up": me_z - step, "down": me_z + step, "own": me_z}[how]
        flip = 1 if how == "core" else 0
        return ((place + places - step) % places) * cores + (core + flip) % cores

    sends = []
    for t in range(0, nja - 1):
        before = (lambda how: (how, t) if t else ("own", 0))
        sends.append((before("up"), ("up", t + 1), {"ja": me_z + 1}, has_up & (me_z - t >= 0)))
        sends.append((before("down"), ("down", t + 1), {"ja": me_z - 1}, has_down & (me_z + t < nja)))
    for t in range(1, places):
        sends.append((("own", 0), ("place", t), placed(t), None))
    if cores == 2:
        for t in range(places):
            sends.append((("place", t) if t else ("own", 0), ("core", t), sibling(), None))

    def copy(it, chunk, number, here, there, device):
        return pltpu.make_async_remote_copy(
            src_ref=buf.at[it, where[here], chunk],
            dst_ref=buf.at[it, where[there], chunk],
            send_sem=send_sem.at[it, number, chunk],
            recv_sem=recv_sem.at[it, where[there], chunk],
            device_id=device,
            device_id_type=MESH,
        )

    def guarded(condition, act):
        if condition is None:
            act()
        else:
            pl.when(condition)(act)

    def send_after(key, it, chunk):
        for number, (here, there, device, condition) in enumerate(sends):
            if here == key:
                guarded(condition, lambda: copy(it, chunk, number, here, there, device).start())

    def take(key, it, chunk):
        copy(it, chunk, 0, key, key, {"ja": me_z, "ia": me_a}).wait_recv()
        send_after(key, it, chunk)

    def send_own(it, c):
        for t in range(nj):
            for f in range(wire.full):
                row = (t * wire.full + f) * size
                buf[it, 0, c, row:row + size] = cur[c, t, :, f * LANES:(f + 1) * LANES]
        for plane in range(wire.shared):
            some = [
                cur[c, t, row:row + wire.piece, wire.full * LANES:] for t, row in wire.pieces(plane)
            ]
            room = LANES - len(some) * wire.rest
            if room:
                some.append(jnp.zeros((wire.piece, room), F32))
            row = wire.low + plane * wire.piece
            buf[it, 0, c, row:row + wire.piece] = jnp.concatenate(some, axis=1)
        send_after(("own", 0), it, c)

    greeted = (1 if cores == 2 else 0) + places - 1
    if nja > 1:
        greeted = greeted + has_up.astype(jnp.int32) + has_down.astype(jnp.int32)
    loads[0].wait()
    pl.semaphore_wait(barrier, greeted)
    for c in range(ni):
        send_own(0, c)

    for kind, (tiles, coup, counts, count) in enumerate(
        ((row_tiles, row_coup, row_counts, ni), (col_tiles, col_coup, col_counts, nj))
    ):
        for a in range(count):
            def fill(k, carry, kind=kind, tiles=tiles, coup=coup, counts=counts, a=a):
                slot, weight = jnp.int32(0), F32(0)
                live = counts[a]
                for l in range(slots):
                    match = tiles[a, l] == k
                    slot = jnp.where(match, jnp.int32(l), slot)
                    weight = jnp.where(match & (l < live), coup[a, l], weight)
                slot_tab[kind, a, k] = slot
                weight_tab[kind, a, k] = weight
                return carry

            lax.fori_loop(0, norbs[kind], fill, 0)

    rows_of = lax.broadcasted_iota(jnp.int32, (size, size), 0)
    columns_of = lax.broadcasted_iota(jnp.int32, (size, size), 1)
    for i in range(ni):
        for j in range(nj):
            across = virt[i, j:j + 1, :]
            down = jnp.sum(jnp.where(rows_of == columns_of, across, 0.0), axis=1, keepdims=True)
            den[i, j] = down + across - first[i] - second[j]
            acc[i, j] = jnp.zeros((size, size), F32)

    for load in loads[1:]:
        load.wait()

    flat = [event for group in groups for event in group]

    def pick(e, values):
        out = values[0]
        for index in range(1, len(values)):
            if values[index] is not values[index - 1]:
                out = jnp.where(e >= index, values[index], out)
        return out

    def one_event(it, e):
        start = 0
        for group in groups:
            def take_group(group=group):
                for kind, how, step, chunk in group:
                    guarded(here_of(how, step), lambda: take((how, step), it, chunk))

            if group[0][1] != "own":
                pl.when(e == start)(take_group)
            start += len(group)

        kind = pick(e, [jnp.int32(event[0] == "col") for event in flat])
        index = pick(e, [jnp.int32(where[event[1], event[2]]) for event in flat])
        chunk = pick(e, [jnp.int32(event[3]) for event in flat])
        source = pick(e, [source_of(*event[:3]) for event in flat])
        present = [here_of(event[1], event[2]) for event in flat]
        here = pick(e, [jnp.int32(1) if x is None else x.astype(jnp.int32) for x in present]) > 0

        @pl.when(here)
        def _():
            for t in range(nj):
                for f in range(wire.full):
                    lanes = slice(f * LANES, (f + 1) * LANES)
                    row = (t * wire.full + f) * size
                    t_high[t, :, lanes], t_low[t, :, lanes] = split(buf[it, index, chunk, row:row + size])
            for plane in range(wire.shared):
                low = wire.low + plane * wire.piece
                part = buf[it, index, chunk, low:low + wire.piece]
                for q, (t, row) in enumerate(wire.pieces(plane)):
                    mine = pltpu.roll(part, LANES - q * wire.rest, 1) if q else part
                    high, low_part = split(mine[:, :wire.rest])
                    t_high[t, row:row + wire.piece, wire.full * LANES:] = high
                    t_low[t, row:row + wire.piece, wire.full * LANES:] = low_part

            is_row = kind == 0

            def products(a):
                orbital = jnp.where(is_row, source * ni + chunk, source * nj + a)
                i = jnp.where(is_row, a, chunk)
                out = []
                for j in range(nj):
                    mine = jnp.where(is_row, a, j)
                    tile = jnp.where(is_row, j, a)
                    slot = slot_tab[kind, mine, orbital]
                    weight = weight_tab[kind, mine, orbital]
                    s_high, s_low = split(s_all[kind, i, j, slot])
                    x = dot(jnp.concatenate([s_high, s_low], axis=0), t_high[tile], 0)
                    x = x[:size] + x[size:] + dot(s_high, t_low[tile], 0)
                    out.append((i, j, x * weight, s_high, s_low))
                return out

            def finish(out):
                for i, j, x, s_high, s_low in out:
                    acc[i, j] += product3(x, s_high, s_low, 1)

            if ni == nj:
                some = [products(a) for a in range(ni)]
                for out in some:
                    finish(out)
            else:
                def one(a, carry):
                    finish(products(a))
                    return carry

                lax.fori_loop(0, jnp.where(is_row, ni, nj), one, 0)

    def one_iteration(it, carry):
        def step(e, inner):
            one_event(it, e)
            return inner

        lax.fori_loop(0, len(flat), step, 0)

        @pl.when(it < ITERS - 1)
        def _():
            for i in range(ni):
                for j in range(nj):
                    residual = given[i, j] + den[i, j] * cur[i, j] - acc[i, j]
                    cur[i, j] = cur[i, j] - residual / den[i, j]
                    acc[i, j] = jnp.zeros((size, size), F32)
                send_own(it + 1, i)

        return carry

    lax.fori_loop(0, ITERS, one_iteration, 0)

    def drain(it, carry):
        for number, (here, there, device, condition) in enumerate(sends):
            for chunk in range(ni):
                guarded(condition, lambda: copy(it, chunk, number, here, there, device).wait_send())
        return carry

    lax.fori_loop(0, ITERS, drain, 0)


def local(
    nia, nja,
    amplitudes, integrals, row_intersection, column_intersection, row_tiles, row_coupling, row_counts,
    column_tiles, column_coupling, column_counts, virtual_energy, first_energy, second_energy,
):
    ni, nj, size, _ = amplitudes.shape
    wire = Wire(nj, size)
    cores, places, groups = events_of(ni, nia, nja)
    buffers = len(buffers_of(cores, places, nja))
    number_sends = 2 * (nja - 1) + (places - 1) + (places if cores == 2 else 0)
    norb = max(nia * ni, nja * nj)
    vmem = pl.BlockSpec(memory_space=pltpu.VMEM)
    smem = pl.BlockSpec(memory_space=pltpu.SMEM)
    anywhere = pl.BlockSpec(memory_space=pl.ANY)
    flops = 2 * 2 * 3 * size**3 * ni * nj * 2 * norb * ITERS
    shape = jax.ShapeDtypeStruct(amplitudes.shape, F32)
    current, terms = pl.pallas_call(
        functools.partial(kernel, nia, nja, wire),
        out_shape=(shape, shape),
        in_specs=[smem] * 6 + [vmem, smem, smem] + [anywhere] * 4,
        out_specs=(vmem, vmem),
        scratch_shapes=[
            pltpu.VMEM((2,) + row_intersection.shape, F32),
            pltpu.VMEM((ITERS, buffers, ni, wire.rows, LANES), F32),
            pltpu.VMEM(amplitudes.shape, F32),
            pltpu.VMEM(amplitudes.shape, F32),
            pltpu.VMEM((nj, size, size), BF16),
            pltpu.VMEM((nj, size, size), BF16),
            pltpu.SMEM((2, max(ni, nj), norb), jnp.int32),
            pltpu.SMEM((2, max(ni, nj), norb), F32),
            pltpu.SemaphoreType.DMA((4,)),
            pltpu.SemaphoreType.DMA((ITERS, max(number_sends, 1), ni)),
            pltpu.SemaphoreType.DMA((ITERS, buffers, ni)),
        ],
        compiler_params=pltpu.CompilerParams(
            collective_id=0, has_side_effects=True, vmem_limit_bytes=60 * 1024 * 1024
        ),
        cost_estimate=pl.CostEstimate(flops=flops, bytes_accessed=2 * row_intersection.size * 4, transcendentals=0),
        name="pair_residual",
    )(
        row_tiles, row_coupling, row_counts, column_tiles, column_coupling, column_counts, virtual_energy,
        first_energy, second_energy, amplitudes, integrals, row_intersection, column_intersection,
    )
    denom = (
        virtual_energy[:, :, :, None]
        + virtual_energy[:, :, None, :]
        - first_energy[:, None, None, None]
        - second_energy[None, :, None, None]
    )
    residual = integrals + denom * current - terms
    return current - residual / denom, residual


def solution(mesh):
    pair = P(("grp", "ia"), "ja", None, None)
    placed = (
        pair,
        pair,
        P(("grp", "ia"), "ja", None, None, None),
        P(("grp", "ia"), "ja", None, None, None),
        P(("grp", "ia"), None),
        P(("grp", "ia"), None),
        P(("grp", "ia")),
        P(("grp", "ja"), None),
        P(("grp", "ja"), None),
        P(("grp", "ja")),
        P(("grp", "ia"), "ja", None),
        P(("grp", "ia")),
        P(("grp", "ja")),
    )
    return jax.shard_map(
        functools.partial(local, mesh.shape["ia"], mesh.shape["ja"]),
        mesh=mesh,
        in_specs=placed,
        out_specs=(pair, pair),
        check_vma=False,
    )
```

time: 68.4 us -> 65.1 us (0.952)
  local copies, waits for them, and re-layouts: 3.96 us -> 0.02 us
  other arithmetic: 0 us -> 2.61 us
  Pallas kernels: 63.5 us -> 61.6 us
    unnamed x2 -> x8, local copies, waits for them, and re-layouts: 3.96 us -> 0.02 us
    sub x0 -> x1, other arithmetic: none -> 2.61 us  [local(): return (current - residual / denom, residual)]
    pallas_call x1, Pallas kernels: 63.5 us -> 61.6 us  [local(): pl.pallas_call(functools.partial(kernel, nia, nja, wire), out_shape=(shap...]
where the time goes in v1:
time: 65.1 us; the launch traced here: 64.9 us
  Pallas kernels  61.6 us (95%)
  other arithmetic  2.61 us (4%)
  between operations  0.71 us (1%)
    pallas_call x1, Pallas kernels, local(): pl.pallas_call(functools.partial(kernel, nia, nja, wire), out_shape=(shap...  61.6 us
    sub x1, other arithmetic, local(): return (current - residual / denom, residual)  2.61 us

profile of v1, /device:TPU:0, one launch (start us, length us, event | category | flops | bytes accessed | tf_op | source)
XLA Modules:
  0.0 64.9 jit_solution(13960555976147732367)
XLA Ops:
  0.6 0.0 copy-start.3
  0.6 0.0 copy-start.2
  0.7 0.0 copy-start.1
  0.7 0.0 copy-start
  0.7 61.6 %pair_residual.1 = (f32[2,2,160,160]{3,2,1,0:T(8,128)}, f32[2,2,160,160]{3,2,1,0:T(8,128)}) custom-call(s32[2,8]{1,0:T(2,128)} %row_tiles.1, f32[2,8]{1,0:T(2,128)} %row_coup.1, s32[2]{0:T(128)} %row_counts.1, s32[2,8]{1,0:T(2,128)} %col_tiles.1, f32[2,8]{1,0:T(2,128)} %col_coup.1, s32[2]{0:T(128)} %col_counts.1, f32[2,2,160]{2,1,0:T(2,128)} %virt.1, ...), custom_call_target="tpu_custom_call" | custom-call | flops 6291456000 | bytes 6553600 | tf_op jit(solution)/shard_map/pair_residual/pallas_call | solution.py:348
  62.2 0.0 copy-done.3
  62.3 0.0 copy-done.2
  62.3 0.0 copy-done.1
  62.3 0.0 copy-done
  62.3 2.6 %divide_subtract_fusion = (f32[2,2,160,160]{3,2,1,0:T(8,128)}, f32[2,2,160,160]{3,2,1,0:T(8,128)}) fusion(f32[2,2,160,160]{3,2,1,0:T(8,128)} %get-tuple-element.4, f32[2]{0:T(128)S(1)} %copy-done.3, f32[2]{0:T(128)S(1)} %copy-done.2, f32[2,2,160]{2,1,0:T(2,128)S(1)} %copy-done.1, f32[2,2,160,160]{3,2,1,0:T(8,128)} %get-tuple-element.5, ...), kind=kLoop, calls=%fused_computation | loop fusion | flops 819200 | bytes 2050576 | tf_op jit(solution)/shard_map/sub | solution.py:382
Async XLA Ops:
  0.6 61.6 %copy-start.3 = (f32[2]{0:T(128)S(1)}, f32[2]{0:T(128)}, u32[]{:S(2)}) copy-start(f32[2]{0:T(128)} %second.1) | copy-start | bytes 28
  0.6 61.6 %copy-start.2 = (f32[2]{0:T(128)S(1)}, f32[2]{0:T(128)}, u32[]{:S(2)}) copy-start(f32[2]{0:T(128)} %first.1) | copy-start | bytes 28
  0.7 61.6 %copy-start.1 = (f32[2,2,160]{2,1,0:T(2,128)S(1)}, f32[2,2,160]{2,1,0:T(2,128)}, u32[]{:S(2)}) copy-start(f32[2,2,160]{2,1,0:T(2,128)} %virt.1) | copy-start | bytes 7684
  0.7 61.6 %copy-start = (f32[2,2,160,160]{3,2,1,0:T(8,128)S(1)}, f32[2,2,160,160]{3,2,1,0:T(8,128)}, u32[]{:S(2)}) copy-start(f32[2,2,160,160]{3,2,1,0:T(8,128)} %integ.1) | copy-start | bytes 1228804

commit v2 on v1

--- a/solution.py
+++ b/solution.py
@@ -344,7 +344,7 @@
     smem = pl.BlockSpec(memory_space=pltpu.SMEM)
     anywhere = pl.BlockSpec(memory_space=pl.ANY)
     flops = 2 * 2 * 3 * size**3 * ni * nj * 2 * norb * ITERS
-    shape = jax.ShapeDtypeStruct(amplitudes.shape, F32)
+    shape = pltpu.VMEM(amplitudes.shape, F32)
     current, terms = pl.pallas_call(
         functools.partial(kernel, nia, nja, wire),
         out_shape=(shape, shape),

time: 65.1 us -> 62.7 us (0.963)
  other arithmetic: 2.61 us -> 1.32 us
  Pallas kernels: 61.6 us -> 60.5 us
    sub x1, other arithmetic: 2.61 us -> 1.32 us  [local(): return (current - residual / denom, residual)]
    pallas_call x1, Pallas kernels: 61.6 us -> 60.5 us  [local(): pl.pallas_call(functools.partial(kernel, nia, nja, wire), out_shape=(shap...]
where the time goes in v2:
time: 62.7 us; the launch traced here: 62.6 us
  Pallas kernels  60.5 us (96%)
  other arithmetic  1.32 us (2%)
  between operations  0.71 us (1%)
    pallas_call x1, Pallas kernels, local(): pl.pallas_call(functools.partial(kernel, nia, nja, wire), out_shape=(shap...  60.5 us
    sub x1, other arithmetic, local(): return (current - residual / denom, residual)  1.32 us

profile of v2, /device:TPU:0, one launch (start us, length us, event | category | flops | bytes accessed | tf_op | source)
XLA Modules:
  0.0 62.6 jit_solution(15204519155477648245)
XLA Ops:
  0.6 0.0 copy-start.3
  0.6 0.0 copy-start.2
  0.7 0.0 copy-start.1
  0.7 0.0 copy-start
  0.7 60.5 %pair_residual.1 = (f32[2,2,160,160]{3,2,1,0:T(8,128)S(1)}, f32[2,2,160,160]{3,2,1,0:T(8,128)S(1)}) custom-call(s32[2,8]{1,0:T(2,128)} %row_tiles.1, f32[2,8]{1,0:T(2,128)} %row_coup.1, s32[2]{0:T(128)} %row_counts.1, s32[2,8]{1,0:T(2,128)} %col_tiles.1, f32[2,8]{1,0:T(2,128)} %col_coup.1, s32[2]{0:T(128)} %col_counts.1, f32[2,2,160]{2,1,0:T(2,128)} %virt.1, ...), custom_call_target="tpu_custom_call" | custom-call | flops 6291456000 | bytes 6553600 | tf_op jit(solution)/shard_map/pair_residual/pallas_call | solution.py:348
  61.2 0.0 copy-done.3
  61.2 0.0 copy-done.2
  61.2 0.0 copy-done.1
  61.2 0.0 copy-done
  61.2 1.3 %divide_subtract_fusion = (f32[2,2,160,160]{3,2,1,0:T(8,128)}, f32[2,2,160,160]{3,2,1,0:T(8,128)}) fusion(f32[2,2,160,160]{3,2,1,0:T(8,128)S(1)} %get-tuple-element.4, f32[2]{0:T(128)S(1)} %copy-done.3, f32[2]{0:T(128)S(1)} %copy-done.2, f32[2,2,160]{2,1,0:T(2,128)S(1)} %copy-done.1, f32[2,2,160,160]{3,2,1,0:T(8,128)S(1)} %get-tuple-element.5, ...), kind=kLoop, calls=%fused_computation | loop fusion | flops 819200 | bytes 2050576 | tf_op jit(solution)/shard_map/sub | solution.py:382
Async XLA Ops:
  0.6 60.6 %copy-start.3 = (f32[2]{0:T(128)S(1)}, f32[2]{0:T(128)}, u32[]{:S(2)}) copy-start(f32[2]{0:T(128)} %second.1) | copy-start | bytes 28
  0.6 60.6 %copy-start.2 = (f32[2]{0:T(128)S(1)}, f32[2]{0:T(128)}, u32[]{:S(2)}) copy-start(f32[2]{0:T(128)} %first.1) | copy-start | bytes 28
  0.7 60.6 %copy-start.1 = (f32[2,2,160]{2,1,0:T(2,128)S(1)}, f32[2,2,160]{2,1,0:T(2,128)}, u32[]{:S(2)}) copy-start(f32[2,2,160]{2,1,0:T(2,128)} %virt.1) | copy-start | bytes 7684
  0.7 60.6 %copy-start = (f32[2,2,160,160]{3,2,1,0:T(8,128)S(1)}, f32[2,2,160,160]{3,2,1,0:T(8,128)}, u32[]{:S(2)}) copy-start(f32[2,2,160,160]{3,2,1,0:T(8,128)} %integ.1) | copy-start | bytes 1228804
